TPU v7x, 768 devices: a whole 4x8x12 slice. The times are simulated.
768 devices in a mesh: fsdp: 24 (over z, core), rep: 32 (over x, y).
Axes of the slice: x: 4, y: 8, z: 12, core: 2. Of those that a mesh axis runs over, the one named last changes fastest.
Arguments:
- grad_partial: bfloat16 [32, 144, 512, 512], P('rep', 'fsdp'), may hold values from -3 to 3
- basis_left: bfloat16 [144, 512, 512], P('fsdp'), may hold values from -0.25 to 0.25
- basis_right: bfloat16 [144, 512, 512], P('fsdp'), may hold values from -0.25 to 0.25
- owner_table: int32 [144], replicated, may hold values from 0 to 23, as said below
- moment_first: bfloat16 [24, 12, 512, 512], P('fsdp', None, 'rep'), may hold values from -6 to 6
- moment_second: float32 [24, 12, 512, 512], P('fsdp', None, 'rep'), may hold values from 0.1 to 10
Outputs:
- update: bfloat16 [144, 512, 512], P('fsdp', 'rep')
- new_first: bfloat16 [24, 12, 512, 512], P('fsdp', None, 'rep')
- new_second: float32 [24, 12, 512, 512], P('fsdp', None, 'rep')
Inputs may be any that keep to these rules, and one draw needn't show every extreme that they name: `owner_table`: block b belongs to the shard of fsdp index b // 6. At most 1 block of one shard name the same owner, and at most 12 blocks in all name the same owner; both bounds are reached in every draw.
All inputs are finite; a program needn't handle non-finite values.
Results may differ from a plain program's by a relative error of at most 0.015.
Values may be sent and summed in bfloat16 or wider, within the bound.
A program may use at most 64 MiB of HBM per device.

v0:
```python
import jax
import jax.numpy as jnp
from jax import lax
from jax.sharding import PartitionSpec as P

BETA_ONE = 0.9
BETA_TWO = 0.95
EPSILON = 1e-08


def block_ranks(owner_table, shard_blocks):
    position = jnp.arange(owner_table.shape[0], dtype=jnp.int32)
    same_owner = owner_table[:, None] == owner_table[None, :]
    earlier = position[None, :] < position[:, None]
    source = position // shard_blocks
    same_shard = source[:, None] == source[None, :]
    owner_rank = jnp.sum((same_owner & earlier).astype(jnp.int32), axis=1)
    pair_slot = jnp.sum((same_owner & earlier & same_shard).astype(jnp.int32), axis=1)
    return (source, owner_rank, pair_slot)


def one_hot(values, length):
    return (values[:, None] == jnp.arange(length, dtype=jnp.int32)[None, :]).astype(jnp.bfloat16)


def body(grad_partial, basis_left, basis_right, owner_table, moment_first, moment_second):
    shard_count = lax.axis_size("fsdp")
    replicas = lax.axis_size("rep")
    shard_blocks = basis_left.shape[0]
    block_size = basis_left.shape[1]
    block_rows = block_size // replicas
    owner_slots = moment_first.shape[1]
    pair_slots = (owner_slots + shard_count - 1) // shard_count
    shard_index = lax.axis_index("fsdp")
    replica_index = lax.axis_index("rep")
    right_part = jnp.einsum(
        "kij,kjl->kil", grad_partial[0], basis_right, preferred_element_type=jnp.float32
    ).astype(jnp.bfloat16)
    rotated = lax.psum_scatter(
        jnp.einsum(
            "kji,kjl->ikl", basis_left, right_part, preferred_element_type=jnp.float32
        ).astype(jnp.bfloat16),
        "rep",
        scatter_dimension=0,
        tiled=True,
    )
    source, owner_rank, pair_slot = block_ranks(owner_table, shard_blocks)
    local_owner = lax.dynamic_slice_in_dim(owner_table, shard_index * shard_blocks, shard_blocks)
    local_pair = lax.dynamic_slice_in_dim(pair_slot, shard_index * shard_blocks, shard_blocks)
    chooser = (
        one_hot(local_owner, shard_count)[:, :, None] * one_hot(local_pair, pair_slots)[:, None, :]
    )
    is_mine = (owner_table == shard_index).astype(jnp.bfloat16)
    slot_hot = one_hot(owner_rank, owner_slots) * is_mine[:, None]
    placing = jnp.einsum(
        "bs,bc,bj->scj",
        one_hot(source, shard_count),
        one_hot(pair_slot, pair_slots),
        slot_hot,
        preferred_element_type=jnp.float32,
    ).astype(jnp.bfloat16)
    outgoing = jnp.einsum(
        "kot,rkl->otrl", chooser, rotated, preferred_element_type=jnp.float32
    ).astype(jnp.bfloat16)
    incoming = lax.all_to_all(outgoing, "fsdp", split_axis=0, concat_axis=0, tiled=True)
    arrived = jnp.einsum("stj,strl->jrl", placing, incoming, preferred_element_type=jnp.float32)
    filled = jnp.sum(slot_hot.astype(jnp.float32), axis=0)[:, None, None] > 0.5
    first_old = moment_first[0].astype(jnp.float32)
    second_old = moment_second[0]
    first_new = BETA_ONE * first_old + (1.0 - BETA_ONE) * arrived
    second_new = BETA_TWO * second_old + (1.0 - BETA_TWO) * arrived * arrived
    direction = (first_new / (jnp.sqrt(second_new) + EPSILON)).astype(jnp.bfloat16)
    new_first = jnp.where(filled, first_new.astype(jnp.bfloat16), moment_first[0])[None]
    new_second = jnp.where(filled, second_new, second_old)[None]
    returning = jnp.einsum(
        "stj,jrl->strl", placing, direction, preferred_element_type=jnp.float32
    ).astype(jnp.bfloat16)
    returned = lax.all_to_all(returning, "fsdp", split_axis=0, concat_axis=0, tiled=True)
    direction_rows = jnp.einsum(
        "kot,otrl->rkl", chooser, returned, preferred_element_type=jnp.float32
    ).astype(jnp.bfloat16)
    left_rows = lax.dynamic_slice_in_dim(basis_left, replica_index * block_rows, block_rows, 1)
    left_back = jnp.einsum(
        "kac,ckl->akl",
        left_rows,
        lax.all_gather(direction_rows, "rep", axis=0, tiled=True),
        preferred_element_type=jnp.float32,
    ).astype(jnp.bfloat16)
    update = jnp.einsum(
        "akl,kml->kam", left_back, basis_right, preferred_element_type=jnp.float32
    ).astype(jnp.bfloat16)
    return (update, new_first, new_second)


def solution(mesh):
    placed = (
        P("rep", "fsdp", None, None),
        P("fsdp", None, None),
        P("fsdp", None, None),
        P(),
        P("fsdp", None, "rep", None),
        P("fsdp", None, "rep", None),
    )
    return jax.shard_map(
        body,
        mesh=mesh,
        in_specs=placed,
        out_specs=(
            P("fsdp", "rep", None),
            P("fsdp", None, "rep", None),
            P("fsdp", None, "rep", None),
        ),
        check_vma=False,
    )
```

profile of v0, /device:TPU:1, one launch (start us, length us, event | category | flops | bytes accessed | tf_op | source)
XLA Modules:
  0.0 415.4 jit_solution(10510318317413236560)
XLA Ops:
  7.2 0.0 copy-start
  7.2 0.0 reduce-scatter.2.cloned.1.call-start
  7.2 1.8 copy-done
  9.1 7.9 %convert_bitcast_fusion = bf16[512,6,512]{0,2,1:T(8,128)(2,1)} fusion(bf16[6,512,512]{2,1,0:T(8,128)(2,1)} %param.7, bf16[6,512,512]{2,1,0:T(8,128)(2,1)S(1)} %copy-done, bf16[1,6,512,512]{3,2,1,0:T(8,128)(2,1)} %param.6), kind=kOutput, calls=%fused_computation.2 | convolution fusion | flops 3224371200 | bytes 12582912 | tf_op jit(solution)/shard_map/kji,kjl->ikl/dot_general | solution.py:40
  17.0 7.7 %copy.33 = bf16[512,6,512]{2,1,0:T(8,128)(2,1)} copy(bf16[512,6,512]{0,2,1:T(8,128)(2,1)} %convert_bitcast_fusion) | data formatting | bytes 6291456 | tf_op jit(solution)/shard_map/convert_element_type | solution.py:42
  24.7 0.0 copy-start.3
  24.8 0.0 reduce-scatter.2.cloned.1.call-update
  24.8 0.6 copy-done.3
  25.4 0.1 dynamic_slice.9
  25.5 0.0 copy-start.6
  25.5 0.2 convert_reduce_fusion.1
  25.8 0.1 compare_convert_fusion
  25.8 0.0 copy-start.8
  25.8 234.1 %reduce-scatter.2.cloned.1.call-done = bf16[16,6,512]{2,1,0:T(8,128)(2,1)} async-done(((bf16[512,6,512]{2,1,0:T(8,128)(2,1)}), bf16[16,6,512]{2,1,0:T(8,128)(2,1)}) %reduce-scatter.2.cloned.1.call-update) | async-done | bytes 98320 | tf_op jit(solution)/shard_map/reduce_scatter | solution.py:39
  260.0 1.3 fusion.10
  261.2 0.9 copy.34
  262.1 0.0 copy-done.6
  262.1 0.0 copy-done.8
  262.1 15.2 %all-to-all-start = ((bf16[24,1,16,512]{3,2,1,0:T(8,128)(2,1)}), bf16[24,1,16,512]{3,2,1,0:T(8,128)(2,1)S(1)}, u32[]{:S(2)}, u32[]{:S(2)}) async-start(bf16[24,1,16,512]{3,2,1,0:T(8,128)(2,1)} %copy.34), calls=%async_computation.1 | async-start | bytes 786432 | tf_op jit(solution)/shard_map/all_to_all | solution.py:65
  277.4 0.0 all-gather.2.cloned.1.call-start
  277.4 0.0 copy-start.4
  277.4 0.0 copy-start.7
  277.4 0.5 copy-done.4
  277.9 0.2 fusion.14
  278.1 0.0 copy-start.5
  278.1 17.4 %all-to-all-done = bf16[24,1,16,512]{3,2,1,0:T(8,128)(2,1)S(1)} async-done(((bf16[24,1,16,512]{3,2,1,0:T(8,128)(2,1)}), bf16[24,1,16,512]{3,2,1,0:T(8,128)(2,1)S(1)}, u32[]{:S(2)}, u32[]{:S(2)}) %all-to-all-start) | async-done | bytes 393248 | tf_op jit(solution)/shard_map/all_to_all | solution.py:65
  295.6 0.0 copy-start.9
  295.6 0.4 fusion.18
  296.0 0.0 copy-start.1
  296.0 0.8 copy-done.1
  296.8 0.0 copy-start.2
  296.8 1.7 fusion.11
  298.6 0.1 copy.37
  298.7 23.9 %all_to_all.10 = bf16[24,1,16,512]{3,2,1,0:T(8,128)(2,1)S(1)} all-to-all(bf16[24,1,16,512]{3,2,1,0:T(8,128)(2,1)S(1)} %copy.37), channel_id=1, replica_groups=mesh['fsdp'=24,'rep'=32] {'fsdp'}, dimensions={0} | all-to-all | bytes 786432 | tf_op jit(solution)/shard_map/all_to_all | solution.py:78
  322.6 0.0 copy-done.7
  322.6 0.0 copy-done.9
  322.6 0.3 fusion.12
  322.9 0.7 copy.39
  323.6 0.0 all-gather.2.cloned.1.call-update
  323.6 0.0 copy-done.5
  323.6 0.1 convert_reduce_fusion.2
  323.8 0.0 copy-done.2
  323.8 1.4 fusion.16
  325.1 1.0 copy.41
  326.1 1.3 fusion.24
  327.4 0.8 copy.40
  328.2 76.4 %all-gather.2.cloned.1.call-done = bf16[512,6,512]{2,0,1:T(8,128)(2,1)} async-done(((bf16[16,6,512]{2,0,1:T(8,128)(2,1)}), bf16[512,6,512]{2,0,1:T(8,128)(2,1)}) %all-gather.2.cloned.1.call-update) | async-done | bytes 3145744 | tf_op jit(solution)/shard_map/all_gather | solution.py:86
  404.6 3.9 convolution_convert_fusion.4
  (3 shorter events, 0.0 us)
Async XLA Ops:
  7.2 1.9 copy-start
  7.2 252.8 %reduce-scatter.2.cloned.1.call-start = ((), (), s32[]{:S(2)}) async-start(), calls=%async_computation.3 | async-start | bytes 4325376 | tf_op jit(solution)/shard_map/reduce_scatter | solution.py:39
  24.7 0.7 copy-start.3
  25.5 236.6 %copy-start.6 = (s32[6]{0:T(128)}, s32[6]{0:T(128)S(1)}, u32[]{:S(2)}) copy-start(s32[6]{0:T(128)S(1)} %dynamic_slice.9) | copy-start | bytes 76
  25.8 236.3 %copy-start.8 = (bf16[6]{0:T(256)(128)(2,1)}, bf16[6]{0:T(256)(128)(2,1)S(1)}, u32[]{:S(2)}) copy-start(bf16[6]{0:T(256)(128)(2,1)S(1)} %compare_convert_fusion) | copy-start | bytes 40
  262.1 33.5 %all-to-all-start = ((bf16[24,1,16,512]{3,2,1,0:T(8,128)(2,1)}), bf16[24,1,16,512]{3,2,1,0:T(8,128)(2,1)S(1)}, u32[]{:S(2)}, u32[]{:S(2)}) async-start(bf16[24,1,16,512]{3,2,1,0:T(8,128)(2,1)} %copy.34), calls=%async_computation.1 | async-start | bytes 786432 | tf_op jit(solution)/shard_map/all_to_all | solution.py:65
  277.4 127.3 %all-gather.2.cloned.1.call-start = ((), (), s32[]{:S(2)}) async-start(), calls=%async_computation.4 | async-start | bytes 3244032 | tf_op jit(solution)/shard_map/all_gather | solution.py:86
  277.4 0.5 copy-start.4
  277.4 45.2 %copy-start.7 = (s32[6]{0:T(128)S(1)}, s32[6]{0:T(128)}, u32[]{:S(2)}) copy-start(s32[6]{0:T(128)} %copy-done.6) | copy-start | bytes 76
  278.1 45.5 %copy-start.5 = (bf16[144]{0:T(256)(128)(2,1)S(1)}, bf16[144]{0:T(256)(128)(2,1)}, u32[]{:S(2)}) copy-start(bf16[144]{0:T(256)(128)(2,1)} %copy-done.4) | copy-start | bytes 868
  295.6 27.0 %copy-start.9 = (bf16[6]{0:T(256)(128)(2,1)S(1)}, bf16[6]{0:T(256)(128)(2,1)}, u32[]{:S(2)}) copy-start(bf16[6]{0:T(256)(128)(2,1)} %copy-done.8) | copy-start | bytes 40
  296.0 0.8 copy-start.1
  296.8 26.9 %copy-start.2 = (f32[1,12,16,512]{3,2,1,0:T(8,128)S(1)}, f32[1,12,16,512]{3,2,1,0:T(8,128)}, u32[]{:S(2)}) copy-start(f32[1,12,16,512]{3,2,1,0:T(8,128)} %param.11) | copy-start | bytes 1179652
Sparse Core Ops, SparseCore 0:
  24.9 235.0 reduce-scatter.1
  323.7 80.8 all-gather.1
where the time goes:
time: 418 us; the launch traced here: 415 us
  waiting for transfers between devices  328 us (78%)
  blocking collectives  23.9 us (6%)
  matrix products  15.9 us (4%)
  starting transfers between devices  15.3 us (4%)
  local copies, waits for them, and re-layouts  15.1 us (4%)
  between operations  14.2 us (3%)
    reduce_scatter x1, waiting for transfers between devices, body(): lax.psum_scatter(jnp.einsum('kji,kjl->ikl', basis_left, right_part, prefe...  234 us
    all_gather x1, waiting for transfers between devices, body(): lax.all_gather(direction_rows, 'rep', axis=0, tiled=True)  76.4 us
    all_to_all x1, blocking collectives, body(): lax.all_to_all(returning, 'fsdp', split_axis=0, concat_axis=0, tiled=True)  23.9 us
    all_to_all x1, waiting for transfers between devices, body(): lax.all_to_all(outgoing, 'fsdp', split_axis=0, concat_axis=0, tiled=True)  17.4 us
    all_to_all x1, starting transfers between devices, body(): lax.all_to_all(outgoing, 'fsdp', split_axis=0, concat_axis=0, tiled=True)  15.2 us
  transfers between devices with their start and end apart: 3, of which 3 were waited for; matrix products, arithmetic and copies ran while one was open for 1% of the time, Pallas kernels for 0%

commit v1 on v0

v1 whole, which is shorter than its diff:
```python
import functools

import jax
import jax.numpy as jnp
from jax import lax
from jax.experimental import pallas as pl
from jax.experimental.pallas import tpu as pltpu
from jax.sharding import PartitionSpec as P

BETA_ONE = 0.9
BETA_TWO = 0.95
EPSILON = 1e-08
GRID_X = 4
LANES = 128
CHUNKS = 2
F32 = jnp.float32
BF16 = jnp.bfloat16


def kernel(
    sizes,
    grad_hbm,
    left_hbm,
    right_hbm,
    table,
    first_hbm,
    second_hbm,
    update_hbm,
    new_first_hbm,
    new_second_hbm,
    grad,
    left,
    right,
    first,
    second,
    new_first,
    new_second,
    update,
    total_back,
    part,
    ring_a_x,
    ring_a_y,
    ring_b_y,
    ring_b_x,
    reduced,
    outgoing,
    incoming,
    sendback,
    comeback,
    tiles,
    gathered,
    product,
    rows_in,
    slot_table,
    in_sem,
    out_sem,
    ring_send,
    ring_recv,
    swap_send,
    swap_recv,
):
    fsdp, nx, ny, chunks, width, blocks, slots = sizes
    rep = nx * ny
    cols = width // LANES
    half_blocks = blocks // 2
    units = blocks * cols
    shard = lax.axis_index("fsdp")
    replica = lax.axis_index("rep")
    my_x = replica // ny
    my_y = replica % ny

    def at_fsdp(step):
        return {"fsdp": (shard + step) % fsdp}

    def at_rep(step):
        return {"rep": (replica + step) % rep}

    def load(k, which):
        source, target = ((grad_hbm.at[0], grad), (left_hbm, left), (right_hbm, right))[which]
        return pltpu.make_async_copy(source.at[k], target.at[k], in_sem.at[which, k])

    order = [*range(half_blocks, blocks), *range(half_blocks)]
    for k in order:
        for which in (0, 2, 1):
            load(k, which).start()
    load_first = pltpu.make_async_copy(first_hbm.at[0], first, in_sem.at[3, 0])
    load_second = pltpu.make_async_copy(second_hbm.at[0], second, in_sem.at[3, 1])
    load_first.start()
    load_second.start()

    barrier = pltpu.get_barrier_semaphore()

    def greet(axis):
        def body(step, carry):
            pl.semaphore_signal(
                barrier, inc=1, device_id=axis(step), device_id_type=pl.DeviceIdType.MESH
            )
            return carry

        return body

    lax.fori_loop(1, fsdp, greet(at_fsdp), 0)
    lax.fori_loop(1, rep, greet(at_rep), 0)

    def rotate(q, low, high):
        columns = pl.ds(q * width, width)

        def body(k, carry):
            if q == 0:
                for which in (0, 2, 1):
                    load(k, which).wait()
            right_part = jnp.dot(grad[k], right[k, :, columns], preferred_element_type=F32)
            rotated = lax.dot_general(
                left[k],
                right_part.astype(BF16),
                (((0,), (0,)), ((), ())),
                preferred_element_type=F32,
            )
            part[q, k] = rotated.astype(BF16).reshape(nx, ny, 16, width)
            return carry

        lax.fori_loop(low, high, body, 0)

    def remote(source, target, send, recv, device):
        return pltpu.make_async_remote_copy(
            src_ref=source,
            dst_ref=target,
            send_sem=send,
            recv_sem=recv,
            device_id=device,
            device_id_type=pl.DeviceIdType.MESH,
        )

    sent = []

    def ring(count, position, piece, landing, sems, device):
        reach = count // 2
        flying = {}

        def copy(way, step):
            there = (position + way * (reach - step + 1) + count) % count
            side = 0 if way > 0 else 1
            cut = None if step > 1 else side
            return remote(
                piece(there, cut),
                landing(side, step - 1, cut),
                ring_send.at[sems + (side, step - 1)],
                ring_recv.at[sems + (side, step - 1)],
                device(way),
            )

        for step in range(1, reach + 1):
            for way in (1, -1):
                side = 0 if way > 0 else 1
                if step > 1:
                    flying[way].wait_recv()
                    there = (position + way * (reach - step + 1) + count) % count
                    cut = side if step == 2 else None
                    held = piece(there, cut)
                    held[...] = held[...] + landing(side, step - 2, cut)[...]
                flying[way] = copy(way, step)
                flying[way].start()
                sent.append(flying[way])
            yield
        flying[1].wait_recv()
        flying[-1].wait_recv()

    def split(low, count, cut):
        if cut is None:
            return pl.ds(low, count)
        middle = (count + 1) // 2
        return pl.ds(low, middle) if cut == 0 else pl.ds(low + middle, count - middle)

    def along_x(way):
        return {"rep": ((my_x + way + nx) % nx) * ny + my_y}

    def along_y(way):
        return {"rep": my_x * ny + (my_y + way + ny) % ny}

    def total(own, landed):
        return own.astype(F32) + landed[0].astype(F32) + landed[1].astype(F32)

    def sum_a(q):
        mine = pl.ds(0, half_blocks)
        yield from ring(
            nx,
            my_x,
            lambda there, cut: part.at[q, mine, there, split(0, ny, cut)],
            lambda side, step, cut: ring_a_x.at[q, side, step, :, split(0, ny, cut)],
            (q, 0),
            along_x,
        )
        for k in range(half_blocks):
            part[q, k, my_x] = total(
                part[q, k, my_x], [ring_a_x[q, side, nx // 2 - 1, k] for side in (0, 1)]
            ).astype(BF16)
        yield from ring(
            ny,
            my_y,
            lambda there, cut: part.at[q, split(0, half_blocks, cut), my_x, there],
            lambda side, step, cut: ring_a_y.at[q, side, step, split(0, half_blocks, cut)],
            (q, 1),
            along_y,
        )
        for k in range(half_blocks):
            reduced[q, k] = total(
                part[q, k, my_x, my_y], [ring_a_y[q, side, ny // 2 - 1, k] for side in (0, 1)]
            ).astype(BF16)

    def sum_b(q):
        mine = pl.ds(half_blocks, blocks - half_blocks)
        yield from ring(
            ny,
            my_y,
            lambda there, cut: part.at[q, mine, split(0, nx, cut), there],
            lambda side, step, cut: ring_b_y.at[q, side, step, :, split(0, nx, cut)],
            (q, 2),
            along_y,
        )
        for k in range(blocks - half_blocks):
            part[q, half_blocks + k, :, my_y] = total(
                part[q, half_blocks + k, :, my_y],
                [ring_b_y[q, side, ny // 2 - 1, k] for side in (0, 1)],
            ).astype(BF16)
        yield from ring(
            nx,
            my_x,
            lambda there, cut: part.at[
                q, split(half_blocks, blocks - half_blocks, cut), there, my_y
            ],
            lambda side, step, cut: ring_b_x.at[
                q, side, step, split(0, blocks - half_blocks, cut)
            ],
            (q, 3),
            along_x,
        )
        for k in range(blocks - half_blocks):
            reduced[q, half_blocks + k] = total(
                part[q, half_blocks + k, my_x, my_y],
                [ring_b_x[q, side, nx // 2 - 1, k] for side in (0, 1)],
            ).astype(BF16)

    def lookups():
        def of_shard(other, carry):
            rank, picks = carry
            named = jnp.int32(0)
            for k in range(blocks):
                named += (table[other * blocks + k] == shard).astype(jnp.int32)
            slot_table[other] = jnp.minimum(rank, slots - 1)
            away = (shard - other + fsdp) % fsdp
            picks = tuple(
                jnp.where((named > 0) & (rank == j), away, picks[j]) for j in range(slots)
            )
            return rank + named, picks

        count, picks = lax.fori_loop(
            0, fsdp, of_shard, (jnp.int32(0), (jnp.int32(0),) * slots)
        )
        for j in range(slots):
            slot_table[2 * fsdp + j] = picks[j]
        slot_table[2 * fsdp + slots] = count

        def of_owner(owner, carry):
            block = jnp.int32(0)
            for k in range(blocks):
                block = jnp.where(table[shard * blocks + k] == owner, k, block)
            slot_table[fsdp + owner] = block
            return carry

        lax.fori_loop(0, fsdp, of_owner, 0)

    def swap(q, which, source, target):
        def start(step, carry):
            remote(
                source.at[step],
                target.at[step],
                swap_send.at[q, which],
                swap_recv.at[q, which],
                at_fsdp(step),
            ).start()
            return carry

        lax.fori_loop(1, fsdp, start, 0)
        others = pl.ds(1, fsdp - 1)
        whole = remote(
            source.at[others],
            target.at[others],
            swap_send.at[q, which],
            swap_recv.at[q, which],
            at_fsdp(1),
        )
        sent.append(whole)
        return whole

    def to_owners(q):
        def fill(step, carry):
            block = slot_table[fsdp + (shard + step) % fsdp]
            outgoing[q][step] = reduced[q, block]
            return carry

        lax.fori_loop(1, fsdp, fill, 0)
        incoming[q][0] = reduced[q, slot_table[fsdp + shard]]
        return swap(q, 0, outgoing[q], incoming[q])

    def moments(q, arrival):
        arrival.wait_recv()
        columns = pl.ds(q * width, width)
        count = slot_table[2 * fsdp + slots]

        def body(j, carry):
            gradient = incoming[q][slot_table[2 * fsdp + j]].astype(F32)
            first_old = first[j, :, columns].astype(F32)
            second_old = second[j, :, columns]
            first_now = BETA_ONE * first_old + (1.0 - BETA_ONE) * gradient
            second_now = BETA_TWO * second_old + (1.0 - BETA_TWO) * gradient * gradient
            direction[j] = (first_now / (jnp.sqrt(second_now) + EPSILON)).astype(BF16)
            used = j < count
            new_first[j, :, columns] = jnp.where(used, first_now, first_old).astype(BF16)
            new_second[j, :, columns] = jnp.where(used, second_now, second_old)
            return carry

        direction = tiles[1][q]
        lax.fori_loop(0, slots, body, 0)

        def fill(step, carry):
            sendback[q][step] = direction[slot_table[(shard + step) % fsdp]]
            return carry

        lax.fori_loop(1, fsdp, fill, 0)
        comeback[q][0] = direction[slot_table[shard]]
        return swap(q, 1, sendback[q], comeback[q])

    def to_units(q, arrival):
        arrival.wait_recv()
        piece = tiles[0]
        base = q * units

        for k in range(blocks):
            away = (shard - table[shard * blocks + k] + fsdp) % fsdp
            rows = comeback[q][away]
            for c in range(cols):
                piece[base + k * cols + c] = rows[:, c * LANES : (c + 1) * LANES]

        def start(unit, carry):
            @pl.when(unit != replica)
            def _():
                remote(
                    piece.at[unit],
                    gathered.at[replica],
                    swap_send.at[q, 2],
                    swap_recv.at[q, 2],
                    {"rep": unit},
                ).start()

            @pl.when(unit == replica)
            def _():
                gathered[unit] = piece[unit]

            return carry

        lax.fori_loop(base, base + units, start, 0)

    def unit_copy(q, count):
        return remote(
            gathered.at[pl.ds(0, count)],
            gathered.at[pl.ds(0, count)],
            swap_send.at[q, 2],
            swap_recv.at[q, 2],
            at_rep(1),
        )

    def row_copy(q, count):
        return remote(
            product.at[pl.ds(0, count)],
            product.at[pl.ds(0, count)],
            swap_send.at[q, 3],
            swap_recv.at[q, 3],
            at_rep(1),
        )

    def is_unit(q):
        return (replica >= q * units) & (replica < (q + 1) * units)

    def rotate_left(q):
        @pl.when(is_unit(q))
        def _():
            unit_copy(q, rep - 1).wait_recv()
            block = (replica - q * units) // cols
            back = jnp.dot(
                left[block],
                gathered[...].reshape(rep * 16, LANES),
                preferred_element_type=F32,
            )
            product[...] = back.astype(BF16).reshape(rep, 16, LANES)

            def start(step, carry):
                other = (replica + step) % rep
                remote(
                    product.at[other],
                    rows_in.at[replica],
                    swap_send.at[q, 3],
                    swap_recv.at[q, 3],
                    {"rep": other},
                ).start()
                return carry

            lax.fori_loop(1, rep, start, 0)
            rows_in[replica] = product[replica]

    def finish(q):
        @pl.when(is_unit(q))
        def _():
            row_copy(q, units - 1).wait_recv()

        @pl.when(jnp.logical_not(is_unit(q)))
        def _():
            row_copy(q, units).wait_recv()

        base = q * units
        for k in range(blocks):
            rows = jnp.concatenate([rows_in[base + k * cols + c] for c in range(cols)], axis=1)
            back = lax.dot_general(
                rows,
                right[k, :, q * width : (q + 1) * width],
                (((1,), (1,)), ((), ())),
                preferred_element_type=F32,
            )
            if q > 0:
                back = back + total_back[k]
            if q < chunks - 1:
                total_back[k] = back
            else:
                update[k] = back.astype(BF16)

    lookups()
    arrivals = {}
    started = {}

    def begin(q, after=None):
        rotate(q, half_blocks, blocks)
        if after:
            after()
        b = sum_b(q)
        next(b)
        rotate(q, 0, half_blocks)
        a = sum_a(q)
        next(a)
        started[q] = [b, a]

    def advance(q, rounds):
        for _ in range(rounds):
            started[q] = [g for g in started[q] if next(g, True) is None]
        return started[q]

    begin(0, lambda: pl.semaphore_wait(barrier, fsdp + rep - 2))
    for q in range(chunks):
        advance(q, 1)
        if q + 1 < chunks:
            begin(q + 1)
        while advance(q, 1):
            pass
        arrivals[q] = to_owners(q)
        if q == 0:
            load_first.wait()
            load_second.wait()
        if q > 0:
            arrivals[q - 1] = moments(q - 1, arrivals[q - 1])
    arrivals[chunks - 1] = moments(chunks - 1, arrivals[chunks - 1])
    outputs = [
        pltpu.make_async_copy(new_first, new_first_hbm.at[0], out_sem.at[0]),
        pltpu.make_async_copy(new_second, new_second_hbm.at[0], out_sem.at[1]),
    ]
    for copy in outputs:
        copy.start()
    for q in range(chunks):
        to_units(q, arrivals[q])
        rotate_left(q)
        if q > 0:
            finish(q - 1)
    finish(chunks - 1)
    outputs.append(pltpu.make_async_copy(update, update_hbm, out_sem.at[2]))
    outputs[-1].start()

    for copy in sent:
        copy.wait_send()
    for q in range(chunks):

        @pl.when(is_unit(q))
        def _(q=q):
            unit_copy(q, units - 1).wait_send()
            row_copy(q, rep - 1).wait_send()

        @pl.when(jnp.logical_not(is_unit(q)))
        def _(q=q):
            unit_copy(q, units).wait_send()

    for copy in outputs:
        copy.wait()


def body(grad_partial, basis_left, basis_right, owner_table, moment_first, moment_second):
    fsdp = lax.axis_size("fsdp")
    rep = lax.axis_size("rep")
    blocks, size = basis_left.shape[0], basis_left.shape[1]
    slots, rows = moment_first.shape[1], moment_first.shape[2]
    nx = GRID_X
    ny = rep // nx
    width = size // CHUNKS
    half = blocks // 2
    cols = width // LANES
    sizes = (fsdp, nx, ny, CHUNKS, width, blocks, slots)
    anywhere = pl.BlockSpec(memory_space=pl.ANY)

    def vmem(*shape, kind=BF16):
        return pltpu.VMEM(shape, kind)

    tile = (rows, width)
    scratch = [
        vmem(blocks, size, size),
        vmem(blocks, size, size),
        vmem(blocks, size, size),
        vmem(slots, rows, size),
        vmem(slots, rows, size, kind=F32),
        vmem(slots, rows, size),
        vmem(slots, rows, size, kind=F32),
        vmem(blocks, rows, size),
        vmem(blocks, rows, size, kind=F32),
        vmem(CHUNKS, blocks, nx, ny, *tile),
        vmem(CHUNKS, 2, nx // 2, half, ny, *tile),
        vmem(CHUNKS, 2, ny // 2, half, *tile),
        vmem(CHUNKS, 2, ny // 2, blocks - half, nx, *tile),
        vmem(CHUNKS, 2, nx // 2, blocks - half, *tile),
        vmem(CHUNKS, blocks, *tile),
        [vmem(fsdp, *tile) for _ in range(CHUNKS)],
        [vmem(fsdp, *tile) for _ in range(CHUNKS)],
        [vmem(fsdp, *tile) for _ in range(CHUNKS)],
        [vmem(fsdp, *tile) for _ in range(CHUNKS)],
        (
            vmem(CHUNKS * blocks * cols, rows, LANES),
            [vmem(slots, *tile) for _ in range(CHUNKS)],
        ),
        vmem(rep, rows, LANES),
        vmem(rep, rows, LANES),
        vmem(CHUNKS * blocks * cols, rows, LANES),
        pltpu.SMEM((2 * fsdp + slots + 1,), jnp.int32),
        pltpu.SemaphoreType.DMA((4, blocks)),
        pltpu.SemaphoreType.DMA((3,)),
        pltpu.SemaphoreType.DMA((CHUNKS, 4, 2, ny // 2)),
        pltpu.SemaphoreType.DMA((CHUNKS, 4, 2, ny // 2)),
        pltpu.SemaphoreType.DMA((CHUNKS, 4)),
        pltpu.SemaphoreType.DMA((CHUNKS, 4)),
    ]
    return pl.pallas_call(
        functools.partial(kernel, sizes),
        out_shape=(
            jax.ShapeDtypeStruct((blocks, rows, size), BF16),
            jax.ShapeDtypeStruct(moment_first.shape, BF16),
            jax.ShapeDtypeStruct(moment_second.shape, F32),
        ),
        in_specs=[
            anywhere,
            anywhere,
            anywhere,
            pl.BlockSpec(memory_space=pltpu.SMEM),
            anywhere,
            anywhere,
        ],
        out_specs=(anywhere,) * 3,
        scratch_shapes=scratch,
        compiler_params=pltpu.CompilerParams(
            collective_id=0, has_side_effects=True, vmem_limit_bytes=56 * 1024 * 1024
        ),
    )(grad_partial, basis_left, basis_right, owner_table, moment_first, moment_second)


def solution(mesh):
    placed = (
        P("rep", "fsdp", None, None),
        P("fsdp", None, None),
        P("fsdp", None, None),
        P(),
        P("fsdp", None, "rep", None),
        P("fsdp", None, "rep", None),
    )
    return jax.shard_map(
        body,
        mesh=mesh,
        in_specs=placed,
        out_specs=(
            P("fsdp", "rep", None),
            P("fsdp", None, "rep", None),
            P("fsdp", None, "rep", None),
        ),
        check_vma=False,
    )
```

time: 418 us -> 108 us (0.26)
  waiting for transfers between devices: 328 us -> 0 us
  Pallas kernels: 0 us -> 101 us
  blocking collectives: 23.9 us -> 0 us
  matrix products: 15.9 us -> 0 us
  starting transfers between devices: 15.3 us -> 0 us
  between operations: 14.2 us -> 0.64 us
  local copies, waits for them, and re-layouts: 15.1 us -> 4.92 us
    reduce_scatter x1 -> x0, waiting for transfers between devices: 234 us -> none  [body(): lax.psum_scatter(jnp.einsum('kji,kjl->ikl', basis_left, right_part, prefe...]
    pallas_call x0 -> x1, Pallas kernels: none -> 101 us  [body(): pl.pallas_call(functools.partial(kernel, sizes), out_shape=(jax.ShapeDtyp...]
    all_gather x1 -> x0, waiting for transfers between devices: 76.4 us -> none  [body(): lax.all_gather(direction_rows, 'rep', axis=0, tiled=True)]
    all_to_all x1 -> x0, blocking collectives: 23.9 us -> none  [body(): lax.all_to_all(returning, 'fsdp', split_axis=0, concat_axis=0, tiled=True)]
    all_to_all x1 -> x0, waiting for transfers between devices: 17.4 us -> none  [body(): lax.all_to_all(outgoing, 'fsdp', split_axis=0, concat_axis=0, tiled=True)]
    dot_general x7 -> x0, matrix products: 15.9 us -> none  [the longest x1 7.94 us: body(): jnp.einsum('kji,kjl->ikl', basis_left, right_part, preferred_element_type...]
    all_to_all x1 -> x0, starting transfers between devices: 15.2 us -> none  [body(): lax.all_to_all(outgoing, 'fsdp', split_axis=0, concat_axis=0, tiled=True)]
    convert_element_type x4 -> x0, local copies, waits for them, and re-layouts: 9.41 us -> none  [the longest x1 7.75 us: body(): rotated = lax.psum_scatter(jnp.einsum('kji,kjl->ikl', basis_left, right_p...]
  transfers between devices with their start and end apart: 3 -> 0, of which waited for: 3 -> 0; matrix products, arithmetic and copies ran while one was open for 1% -> 0% of each run, Pallas kernels for 0% -> 0%
where the time goes in v1:
time: 108 us; the launch traced here: 107 us
  Pallas kernels  101 us (94%)
  local copies, waits for them, and re-layouts  4.92 us (5%)
    pallas_call x1, Pallas kernels, body(): pl.pallas_call(functools.partial(kernel, sizes), out_shape=(jax.ShapeDtyp...  101 us
    unnamed x3, local copies, waits for them, and re-layouts  4.92 us

profile of v1, /device:TPU:1, one launch (start us, length us, event | category | flops | bytes accessed | tf_op | source)
XLA Modules:
  0.0 106.7 jit_solution(15380971831185215273)
XLA Ops:
  0.6 101.1 %shard_map.85 = (bf16[6,16,512]{2,1,0:T(8,128)(2,1)}, bf16[1,12,16,512]{3,2,1,0:T(8,128)(2,1)}, f32[1,12,16,512]{3,2,1,0:T(8,128)}) custom-call(bf16[1,6,512,512]{3,2,1,0:T(8,128)(2,1)} %grad_hbm.1, bf16[6,512,512]{2,1,0:T(8,128)(2,1)} %left_hbm.1, bf16[6,512,512]{2,1,0:T(8,128)(2,1)} %right_hbm.1, s32[144]{0:T(256)} %table.1, ...), custom_call_target="tpu_custom_call" | custom-call | tf_op jit(solution)/shard_map/pallas_call | solution.py:553
  101.8 1.5 %copy.12 = bf16[6,16,512]{2,1,0:T(8,128)(2,1)} copy(bf16[6,16,512]{2,1,0:T(8,128)(2,1)} %get-tuple-element.6) | data formatting | bytes 196608
  103.3 1.6 %copy.13 = bf16[1,12,16,512]{3,2,1,0:T(8,128)(2,1)} copy(bf16[1,12,16,512]{3,2,1,0:T(8,128)(2,1)} %get-tuple-element.7) | data formatting | bytes 393216
  104.9 1.8 %copy.14 = f32[1,12,16,512]{3,2,1,0:T(8,128)} copy(f32[1,12,16,512]{3,2,1,0:T(8,128)} %get-tuple-element.8) | data formatting | bytes 786432
